TPU v7x, 32 devices: a whole 2x2x4 slice. The times are simulated.
32 devices in a mesh: grp: 2 (over y), pts: 8 (over z, x), ctr: 2 (over core).
Axes of the slice: x: 2, y: 2, z: 4, core: 2. Of those that a mesh axis runs over, the one named last changes fastest.
Arguments:
- points: bfloat16 [3072, 128], P(('grp', 'pts')), parts along dimension 0, may hold values from -1.5 to 1.5
- curvature: bfloat16 [3072, 32], P(('grp', 'pts')), parts along dimension 0, may hold values from 0.019897461 to 0.25
- centers: bfloat16 [128, 131072], P(None, ('grp', 'pts', 'ctr')), parts along dimension 1, may hold values from -1.5 to 1.5
- coef: bfloat16 [32, 131072], P(None, ('grp', 'pts', 'ctr')), parts along dimension 1, may hold values from -1.1953125 to 1.1953125
Outputs:
- hvp: float32 [32, 131072], P(None, ('grp', 'pts', 'ctr')), parts along dimension 1
There are 2 independent parts, one for each index of `grp`. A program takes and returns all parts, laid end to end along the dimension named above; each array names one. Nothing has to cross between parts.
All inputs are finite; a program needn't handle non-finite values.
Results may differ from a plain program's by a relative error of at most 0.0003.
Values may be sent and summed in bfloat16 or wider, within the bound.
A program may use at most 64 MiB of HBM per device.

v0:
```python
import jax
import jax.numpy as jnp
from jax import lax
from jax.sharding import PartitionSpec as P


def kernel_tile(points, sq_points, block, scale):
    sq_centers = jnp.sum(jnp.square(block.astype(jnp.float32)), axis=0)
    inner = jnp.dot(points, block, preferred_element_type=jnp.float32)
    dist = sq_points[:, None] + sq_centers[None, :] - 2.0 * inner
    return jnp.exp(-dist * scale).astype(jnp.bfloat16)


def on_device(points, curvature, centers, coef):
    scale = 32.0 / points.shape[1]
    labels = coef.shape[0]
    near_centers, near_coef = (
        lax.all_gather(centers, "pts", axis=1, tiled=True),
        lax.all_gather(coef, "pts", axis=1, tiled=True),
    )
    total = near_centers.shape[1]
    width = total // 4
    sq_points = jnp.sum(jnp.square(points.astype(jnp.float32)), axis=1)
    tangent = jnp.zeros((points.shape[0], labels), jnp.float32)
    for number in range(4):
        block = near_centers[:, number * width : (number + 1) * width]
        tile = kernel_tile(points, sq_points, block, scale)
        values = near_coef[:, number * width : (number + 1) * width]
        tangent = tangent + lax.dot_general(
            tile, values, (((1,), (1,)), ((), ())), preferred_element_type=jnp.float32
        )
    tangent = lax.psum(tangent, "ctr")
    weighted = (curvature.astype(jnp.float32) * tangent).astype(jnp.bfloat16)
    pieces = []
    for number in range(4):
        block = near_centers[:, number * width : (number + 1) * width]
        tile = kernel_tile(points, sq_points, block, scale)
        pieces.append(
            lax.dot_general(
                weighted, tile, (((0,), (0,)), ((), ())), preferred_element_type=jnp.float32
            )
        )
    partial_sum = jnp.concatenate(pieces, axis=1)
    return lax.psum_scatter(partial_sum, "pts", scatter_dimension=1, tiled=True)


def solution(mesh):
    in_specs = (
        P(("grp", "pts"), None),
        P(("grp", "pts"), None),
        P(None, ("grp", "pts", "ctr")),
        P(None, ("grp", "pts", "ctr")),
    )
    out_specs = P(None, ("grp", "pts", "ctr"))
    return jax.shard_map(
        on_device, mesh=mesh, in_specs=in_specs, out_specs=out_specs, check_vma=False
    )
```

profile of v0, /device:TPU:0, one launch (start us, length us, event | category | flops | bytes accessed | tf_op | source)
XLA Modules:
  0.0 299.0 jit_solution(7907585057710424661)
XLA Ops:
  6.5 0.0 all-gather.3.cloned.1.call-start
  6.5 0.7 all-gather.3.cloned.1.call-update
  7.3 0.0 all-gather.5.cloned.1.call-start
  7.3 0.7 all-gather.5.cloned.1.call-update
  8.0 0.0 reduce-scatter.2.cloned.1.call-start
  8.1 0.9 multiply_reduce_fusion.4
  9.0 0.0 copy-start.6
  9.0 128.2 %all-gather.3.cloned.1.call-done = bf16[128,32768]{1,0:T(8,128)(2,1)} async-done(((bf16[128,4096]{1,0:T(8,128)(2,1)}), bf16[128,32768]{1,0:T(8,128)(2,1)}) %all-gather.3.cloned.1.call-update) | async-done | bytes 8388624 | tf_op jit(solution)/shard_map/all_gather | solution.py:18
  137.2 4.5 %multiply_reduce_fusion = (f32[8192]{0:T(1024)S(1)}, f32[8192]{0:T(1024)S(1)}, f32[8192]{0:T(1024)S(1)}, f32[8192]{0:T(1024)S(1)}) fusion(bf16[128,32768]{1,0:T(8,128)(2,1)} %all-gather.3.cloned.1.call-done), kind=kLoop, calls=%fused_computation.25 | loop fusion | flops 12550144 | bytes 8519680 | tf_op jit(solution)/shard_map/reduce_sum | solution.py:8
  141.7 0.0 copy-done.6
  141.7 1.3 copy-done.4
  143.0 1.8 fusion.19
  144.9 3.5 %fusion.18 = bf16[192,8192]{1,0:T(8,128)(2,1)} fusion(bf16[192,128]{1,0:T(8,128)(2,1)S(1)} %copy-done.6, f32[8192]{0:T(1024)S(1)} %get-tuple-element.6, f32[192]{0:T(256)S(1)} %multiply_reduce_fusion.4, bf16[128,32768]{1,0:T(8,128)(2,1)S(1)} %copy-done.4), kind=kOutput, calls=%fused_computation.22 | convolution fusion | flops 412090368 | bytes 5325824 | tf_op jit(solution)/shard_map/dot_general | solution.py:9
  148.4 3.5 %fusion.17 = bf16[192,8192]{1,0:T(8,128)(2,1)} fusion(bf16[192,128]{1,0:T(8,128)(2,1)S(1)} %copy-done.6, f32[8192]{0:T(1024)S(1)} %get-tuple-element.7, f32[192]{0:T(256)S(1)} %multiply_reduce_fusion.4, bf16[128,32768]{1,0:T(8,128)(2,1)S(1)} %copy-done.4), kind=kOutput, calls=%fused_computation.21 | convolution fusion | flops 412090368 | bytes 5325824 | tf_op jit(solution)/shard_map/dot_general | solution.py:9
  151.9 3.5 %fusion.16 = bf16[192,8192]{1,0:T(8,128)(2,1)} fusion(bf16[192,128]{1,0:T(8,128)(2,1)S(1)} %copy-done.6, f32[8192]{0:T(1024)S(1)} %get-tuple-element.8, f32[192]{0:T(256)S(1)} %multiply_reduce_fusion.4, bf16[128,32768]{1,0:T(8,128)(2,1)S(1)} %copy-done.4), kind=kOutput, calls=%fused_computation.20 | convolution fusion | flops 412090368 | bytes 5325824 | tf_op jit(solution)/shard_map/dot_general | solution.py:9
  155.4 31.4 %all-gather.5.cloned.1.call-done = bf16[32,32768]{1,0:T(8,128)(2,1)} async-done(((bf16[32,4096]{1,0:T(8,128)(2,1)}), bf16[32,32768]{1,0:T(8,128)(2,1)}) %all-gather.5.cloned.1.call-update) | async-done | bytes 2097168 | tf_op jit(solution)/shard_map/all_gather | solution.py:19
  186.9 3.2 %fusion.27 = f32[192,32]{0,1:T(8,128)S(1)} fusion(bf16[192,8192]{1,0:T(8,128)(2,1)} %fusion.16, bf16[32,32768]{1,0:T(8,128)(2,1)} %all-gather.5.cloned.1.call-done), kind=kOutput, calls=%fused_computation.39 | convolution fusion | flops 100663296 | bytes 3694592 | tf_op jit(solution)/shard_map/dot_general | solution.py:29
  190.1 3.1 %convolution_add_fusion.2 = f32[192,32]{0,1:T(8,128)S(1)} fusion(f32[192,32]{0,1:T(8,128)S(1)} %fusion.27, bf16[192,8192]{1,0:T(8,128)(2,1)} %fusion.17, bf16[32,32768]{1,0:T(8,128)(2,1)} %all-gather.5.cloned.1.call-done), kind=kOutput, calls=%fused_computation.35 | convolution fusion | flops 100669440 | bytes 3719168 | tf_op jit(solution)/shard_map/dot_general | solution.py:29
  193.2 0.0 copy-start.7
  193.2 1.1 convolution_add_fusion.1
  194.3 1.1 convolution_add_fusion
  195.3 3.4 %psum.7 = f32[192,32]{0,1:T(8,128)S(1)} all-reduce(f32[192,32]{0,1:T(8,128)S(1)} %convolution_add_fusion), channel_id=1, replica_groups=mesh['grp'=2,'pts'=8,'ctr'=2] {'ctr'}, use_global_device_ids=true, to_apply=%region_5.0 | all-reduce | flops 6144 | bytes 49152 | tf_op jit(solution)/shard_map/psum | solution.py:32
  198.8 0.7 fusion.32
  199.5 1.2 copy-done.1
  200.7 0.7 fusion.31
  201.3 0.3 copy-done.2
  201.6 0.7 fusion.30
  202.3 0.5 copy-done.3
  202.8 0.7 fusion.29
  203.5 2.2 pad_maximum_fusion
  205.7 0.0 reduce-scatter.2.cloned.1.call-update
  205.7 86.8 %reduce-scatter.2.cloned.1.call-done = f32[32,4096]{1,0:T(8,128)} async-done(((f32[32,32768]{1,0:T(8,128)}), f32[32,4096]{1,0:T(8,128)}) %reduce-scatter.2.cloned.1.call-update) | async-done | bytes 524304 | tf_op jit(solution)/shard_map/reduce_scatter | solution.py:44
  (10 shorter events, 0.0 us)
Async XLA Ops:
  6.5 130.6 %all-gather.3.cloned.1.call-start = ((), (), s32[]{:S(2)}) async-start(), calls=%async_computation.1 | async-start | bytes 9437184 | tf_op jit(solution)/shard_map/all_gather | solution.py:18
  7.3 179.6 %all-gather.5.cloned.1.call-start = ((), (), s32[]{:S(2)}) async-start(), calls=%async_computation.2 | async-start | bytes 2359296 | tf_op jit(solution)/shard_map/all_gather | solution.py:19
  8.0 284.5 %reduce-scatter.2.cloned.1.call-start = ((), (), s32[]{:S(2)}) async-start(), calls=%async_computation.3 | async-start | bytes 4718592 | tf_op jit(solution)/shard_map/reduce_scatter | solution.py:44
  9.0 132.7 %copy-start.6 = (bf16[192,128]{1,0:T(8,128)(2,1)S(1)}, bf16[192,128]{1,0:T(8,128)(2,1)}, u32[]{:S(2)}) copy-start(bf16[192,128]{1,0:T(8,128)(2,1)} %param.4) | copy-start | bytes 147460
  137.2 5.9 %copy-start.4 = (bf16[128,32768]{1,0:T(8,128)(2,1)S(1)}, bf16[128,32768]{1,0:T(8,128)(2,1)}, u32[]{:S(2)}) copy-start(bf16[128,32768]{1,0:T(8,128)(2,1)} %all-gather.3.cloned.1.call-done) | copy-start | bytes 25165828
  186.9 6.3 %copy-start = (bf16[192,8192]{1,0:T(8,128)(2,1)S(1)}, bf16[192,8192]{1,0:T(8,128)(2,1)}, u32[]{:S(2)}) copy-start(bf16[192,8192]{1,0:T(8,128)(2,1)} %fusion.18) | copy-start | bytes 9437188
  186.9 6.3 %copy-start.5 = (bf16[32,32768]{1,0:T(8,128)(2,1)S(1)}, bf16[32,32768]{1,0:T(8,128)(2,1)}, u32[]{:S(2)}) copy-start(bf16[32,32768]{1,0:T(8,128)(2,1)} %all-gather.5.cloned.1.call-done) | copy-start | bytes 6291460
  193.2 5.6 %copy-start.7 = (bf16[192,32]{0,1:T(8,128)(2,1)S(1)}, bf16[192,32]{0,1:T(8,128)(2,1)}, u32[]{:S(2)}) copy-start(bf16[192,32]{0,1:T(8,128)(2,1)} %param.5) | copy-start | bytes 36868
  198.8 1.9 copy-start.1
  198.8 2.8 copy-start.2
  200.7 2.1 copy-start.3
Sparse Core Ops, SparseCore 0:
  9.5 127.5 all-gather.2
  139.4 47.4 all-gather.4
  205.8 86.5 reduce-scatter.1
where the time goes:
time: 299 us
  waiting for transfers between devices  248 us (83%)
  matrix products  23.5 us (8%)
  between operations  13.2 us (4%)
  other arithmetic  7.63 us (3%)
  blocking collectives  3.41 us (1%)
  local copies, waits for them, and re-layouts  3.29 us (1%)
    all_gather x1, waiting for transfers between devices, on_device(): lax.all_gather(centers, 'pts', axis=1, tiled=True)  128 us
    reduce_scatter x1, waiting for transfers between devices, on_device(): return lax.psum_scatter(partial_sum, 'pts', scatter_dimension=1, tiled=True)  86.8 us
    all_gather x1, waiting for transfers between devices, on_device(): lax.all_gather(coef, 'pts', axis=1, tiled=True)  31.4 us
    dot_general x4, matrix products, kernel_tile(): inner = jnp.dot(points, block, preferred_element_type=jnp.float32)  12.4 us
    dot_general x4, matrix products, on_device(): lax.dot_general(tile, values, (((1,), (1,)), ((), ())), preferred_element...  8.42 us
  transfers between devices with their start and end apart: 3, of which 3 were waited for; matrix products, arithmetic and copies ran while one was open for 6% of the time, Pallas kernels for 0%

commit v1 on v0

--- a/solution.py
+++ b/solution.py
@@ -2,6 +2,19 @@
 import jax.numpy as jnp
 from jax import lax
 from jax.sharding import PartitionSpec as P
+
+
+def gather_around(x, axis, dim):
+    ways = lax.axis_size(axis)
+    up = [(d, (d + 1) % ways) for d in range(ways)]
+    down = [(d, (d - 1) % ways) for d in range(ways)]
+    earlier, later = ([x], [x])
+    for _ in range(ways // 2):
+        earlier.append(lax.ppermute(earlier[-1], axis, up))
+    for _ in range((ways - 1) // 2):
+        later.append(lax.ppermute(later[-1], axis, down))
+    line = jnp.concatenate([*earlier[::-1], *later[1:]], axis=dim)
+    return jnp.roll(line, (lax.axis_index(axis) - ways // 2) * x.shape[dim], axis=dim)
 
 
 def kernel_tile(points, sq_points, block, scale):
@@ -16,7 +29,7 @@
     labels = coef.shape[0]
     near_centers, near_coef = (
         lax.all_gather(centers, "pts", axis=1, tiled=True),
-        lax.all_gather(coef, "pts", axis=1, tiled=True),
+        gather_around(coef, "pts", 1),
     )
     total = near_centers.shape[1]
     width = total // 4

time: 299 us -> 284 us (0.950)
  waiting for transfers between devices: 248 us -> 208 us
  starting transfers between devices: 0.08 us -> 14.3 us
  local copies, waits for them, and re-layouts: 3.29 us -> 14.4 us
    all_gather x1, waiting for transfers between devices: 128 us -> 74.7 us  [on_device(): lax.all_gather(centers, 'pts', axis=1, tiled=True)]
    ppermute x0 -> x7, waiting for transfers between devices: none -> 46.5 us  [the longest x4 42.9 us: gather_around(): earlier.append(lax.ppermute(earlier[-1], axis, up))]
    all_gather x1 -> x0, waiting for transfers between devices: 31.4 us -> none  [on_device(): lax.all_gather(coef, 'pts', axis=1, tiled=True)]
    ppermute x0 -> x7, starting transfers between devices: none -> 14.2 us  [the longest x4 8.54 us: gather_around(): earlier.append(lax.ppermute(earlier[-1], axis, up))]
    unnamed x16 -> x33, local copies, waits for them, and re-layouts: 3.29 us -> 13.7 us
    dot_general x4, matrix products: 12.4 us -> 7.32 us  [kernel_tile(): inner = jnp.dot(points, block, preferred_element_type=jnp.float32)]
  transfers between devices with their start and end apart: 3 -> 9, of which waited for: 3 -> 8; matrix products, arithmetic and copies ran while one was open for 6% -> 5% of each run, Pallas kernels for 0% -> 0%
where the time goes in v1:
time: 284 us; the launch traced here: 283 us
  waiting for transfers between devices  208 us (73%)
  matrix products  21.8 us (8%)
  local copies, waits for them, and re-layouts  14.4 us (5%)
  starting transfers between devices  14.3 us (5%)
  between operations  13.6 us (5%)
  other arithmetic  7.64 us (3%)
  blocking collectives  3.41 us (1%)
    reduce_scatter x1, waiting for transfers between devices, on_device(): return lax.psum_scatter(partial_sum, 'pts', scatter_dimension=1, tiled=True)  86.3 us
    all_gather x1, waiting for transfers between devices, on_device(): lax.all_gather(centers, 'pts', axis=1, tiled=True)  74.7 us
    ppermute x4, waiting for transfers between devices, gather_around(): earlier.append(lax.ppermute(earlier[-1], axis, up))  42.9 us
    unnamed x33, local copies, waits for them, and re-layouts  13.7 us
    dot_general x4, matrix products, on_device(): lax.dot_general(tile, values, (((1,), (1,)), ((), ())), preferred_element...  9.67 us
    ppermute x4, starting transfers between devices, gather_around(): earlier.append(lax.ppermute(earlier[-1], axis, up))  8.54 us
    dot_general x4, matrix products, kernel_tile(): inner = jnp.dot(points, block, preferred_element_type=jnp.float32)  7.32 us
    ppermute x3, starting transfers between devices, gather_around(): later.append(lax.ppermute(later[-1], axis, down))  5.68 us
  transfers between devices with their start and end apart: 9, of which 8 were waited for; matrix products, arithmetic and copies ran while one was open for 5% of the time, Pallas kernels for 0%

profile of v1, /device:TPU:0, one launch (start us, length us, event | category | flops | bytes accessed | tf_op | source)
XLA Modules:
  0.0 283.4 jit_solution(14175212747093213094)
XLA Ops:
  7.3 3.0 %collective-permute-start = (bf16[32,4096]{1,0:T(8,128)(2,1)}, bf16[32,4096]{1,0:T(8,128)(2,1)S(1)}, u32[]{:S(2)}, u32[]{:S(2)}) collective-permute-start(bf16[32,4096]{1,0:T(8,128)(2,1)} %param.7), channel_id=1, source_target_pairs={{0,2},{2,4},{4,6},{6,8},{8,10},{10,12},{12,14},{14,0},{1,3},{3,5},... | collective-permute-start | bytes 786440 | tf_op jit(solution)/shard_map/ppermute | solution.py:13
  10.3 9.6 %collective-permute-done = bf16[32,4096]{1,0:T(8,128)(2,1)S(1)} collective-permute-done((bf16[32,4096]{1,0:T(8,128)(2,1)}, bf16[32,4096]{1,0:T(8,128)(2,1)S(1)}, u32[]{:S(2)}, u32[]{:S(2)}) %collective-permute-start) | collective-permute-done | bytes 262176 | tf_op jit(solution)/shard_map/ppermute | solution.py:13
  19.9 4.7 %collective-permute-start.4 = (bf16[32,4096]{1,0:T(8,128)(2,1)}, bf16[32,4096]{1,0:T(8,128)(2,1)S(1)}, u32[]{:S(2)}, u32[]{:S(2)}) collective-permute-start(bf16[32,4096]{1,0:T(8,128)(2,1)} %param.7), channel_id=1, source_target_pairs={{0,14},{2,0},{4,2},{6,4},{8,6},{10,8},{12,10},{14,12},{1,15},{3,1}... | collective-permute-start | bytes 786440 | tf_op jit(solution)/shard_map/ppermute | solution.py:15
  24.6 11.7 %collective-permute-done.1 = bf16[32,4096]{1,0:T(8,128)(2,1)S(1)} collective-permute-done((bf16[32,4096]{1,0:T(8,128)(2,1)S(1)}, bf16[32,4096]{1,0:T(8,128)(2,1)S(1)}, u32[]{:S(2)}, u32[]{:S(2)}) %collective-permute-start.1) | collective-permute-done | bytes 262176 | tf_op jit(solution)/shard_map/ppermute | solution.py:13
  36.3 3.1 %collective-permute-start.2 = (bf16[32,4096]{1,0:T(8,128)(2,1)S(1)}, bf16[32,4096]{1,0:T(8,128)(2,1)S(1)}, u32[]{:S(2)}, u32[]{:S(2)}) collective-permute-start(bf16[32,4096]{1,0:T(8,128)(2,1)S(1)} %collective-permute-done.1), channel_id=1, source_target_pairs={{0,2},{2,4},{4,6},{6,8},{8,10},{10,12},{12,14},{14,0},{1,3},{3,5},... | collective-permute-start | bytes 786440 | tf_op jit(solution)/shard_map/ppermute | solution.py:13
  39.4 2.2 collective-permute-done.4
  41.6 12.8 %collective-permute-done.2 = bf16[32,4096]{1,0:T(8,128)(2,1)S(1)} collective-permute-done((bf16[32,4096]{1,0:T(8,128)(2,1)S(1)}, bf16[32,4096]{1,0:T(8,128)(2,1)S(1)}, u32[]{:S(2)}, u32[]{:S(2)}) %collective-permute-start.2) | collective-permute-done | bytes 262176 | tf_op jit(solution)/shard_map/ppermute | solution.py:13
  54.4 2.5 collective-permute-start.3
  56.9 0.9 multiply_reduce_fusion.4
  57.8 1.4 collective-permute-done.5
  59.2 0.9 collective-permute-start.6
  60.1 8.9 %collective-permute-done.3 = bf16[32,4096]{1,0:T(8,128)(2,1)S(1)} collective-permute-done((bf16[32,4096]{1,0:T(8,128)(2,1)S(1)}, bf16[32,4096]{1,0:T(8,128)(2,1)S(1)}, u32[]{:S(2)}, u32[]{:S(2)}) %collective-permute-start.3) | collective-permute-done | bytes 262176 | tf_op jit(solution)/shard_map/ppermute | solution.py:13
  69.0 0.7 constant_dynamic-update-slice_fusion.15
  70.4 0.8 constant_dynamic-update-slice_fusion.13
  71.9 1.7 constant_dynamic-update-slice_fusion.11
  78.0 0.8 constant_dynamic-update-slice_fusion.4
  80.9 0.7 constant_dynamic-update-slice_fusion
  81.7 74.7 %all-gather.2.cloned.1.call-done = bf16[128,32768]{1,0:T(8,128)(2,1)} async-done(((bf16[128,4096]{1,0:T(8,128)(2,1)}), bf16[128,32768]{1,0:T(8,128)(2,1)}) %all-gather.2.cloned.1.call-update) | async-done | bytes 8388624 | tf_op jit(solution)/shard_map/all_gather | solution.py:31
  156.4 4.5 %multiply_reduce_fusion.3 = (f32[8192]{0:T(1024)S(1)}, f32[8192]{0:T(1024)S(1)}, f32[8192]{0:T(1024)S(1)}, f32[8192]{0:T(1024)S(1)}) fusion(bf16[128,32768]{1,0:T(8,128)(2,1)} %all-gather.2.cloned.1.call-done), kind=kLoop, calls=%fused_computation.28 | loop fusion | flops 12550144 | bytes 8519680 | tf_op jit(solution)/shard_map/reduce_sum | solution.py:21
  161.0 1.3 copy-done.5
  162.3 1.8 fusion.18
  164.1 2.5 fusion.28
  166.7 1.8 fusion.17
  168.5 2.5 fusion.30
  171.1 1.8 fusion.19
  172.9 2.5 fusion.26
  175.4 1.8 fusion.16
  177.3 2.1 fusion.25
  179.4 3.4 %psum.7 = f32[192,32]{0,1:T(8,128)S(1)} all-reduce(f32[192,32]{0,1:T(8,128)S(1)} %fusion.25), channel_id=1, replica_groups=mesh['grp'=2,'pts'=8,'ctr'=2] {'ctr'}, use_global_device_ids=true, to_apply=%region_5.6 | all-reduce | flops 6144 | bytes 49152 | tf_op jit(solution)/shard_map/psum | solution.py:45
  182.9 2.7 fusion.40
  188.0 2.2 pad_maximum_fusion
  190.3 86.3 %reduce-scatter.2.cloned.1.call-done = f32[32,4096]{1,0:T(8,128)} async-done(((f32[32,32768]{1,0:T(8,128)}), f32[32,4096]{1,0:T(8,128)}) %reduce-scatter.2.cloned.1.call-update) | async-done | bytes 524304 | tf_op jit(solution)/shard_map/reduce_scatter | solution.py:57
  (39 shorter events, 11.3 us)
Async XLA Ops:
  6.5 72.2 %copy-start.6 = (bf16[32,4096]{1,0:T(8,128)(2,1)S(1)}, bf16[32,4096]{1,0:T(8,128)(2,1)}, u32[]{:S(2)}) copy-start(bf16[32,4096]{1,0:T(8,128)(2,1)} %param.7) | copy-start | bytes 786436
  6.5 149.9 %all-gather.2.cloned.1.call-start = ((), (), s32[]{:S(2)}) async-start(), calls=%async_computation.1 | async-start | bytes 9437184 | tf_op jit(solution)/shard_map/all_gather | solution.py:31
  7.3 269.3 %reduce-scatter.2.cloned.1.call-start = ((), (), s32[]{:S(2)}) async-start(), calls=%async_computation.2 | async-start | bytes 4718592 | tf_op jit(solution)/shard_map/reduce_scatter | solution.py:57
  7.3 12.5 %collective-permute-start = (bf16[32,4096]{1,0:T(8,128)(2,1)}, bf16[32,4096]{1,0:T(8,128)(2,1)S(1)}, u32[]{:S(2)}, u32[]{:S(2)}) collective-permute-start(bf16[32,4096]{1,0:T(8,128)(2,1)} %param.7), channel_id=1, source_target_pairs={{0,2},{2,4},{4,6},{6,8},{8,10},{10,12},{12,14},{14,0},{1,3},{3,5},... | collective-permute-start | bytes 786440 | tf_op jit(solution)/shard_map/ppermute | solution.py:13
  19.9 16.4 %collective-permute-start.1 = (bf16[32,4096]{1,0:T(8,128)(2,1)S(1)}, bf16[32,4096]{1,0:T(8,128)(2,1)S(1)}, u32[]{:S(2)}, u32[]{:S(2)}) collective-permute-start(bf16[32,4096]{1,0:T(8,128)(2,1)S(1)} %collective-permute-done), channel_id=1, source_target_pairs={{0,2},{2,4},{4,6},{6,8},{8,10},{10,12},{12,14},{14,0},{1,3},{3,5},... | collective-permute-start | bytes 786440 | tf_op jit(solution)/shard_map/ppermute | solution.py:13
  19.9 21.7 %collective-permute-start.4 = (bf16[32,4096]{1,0:T(8,128)(2,1)}, bf16[32,4096]{1,0:T(8,128)(2,1)S(1)}, u32[]{:S(2)}, u32[]{:S(2)}) collective-permute-start(bf16[32,4096]{1,0:T(8,128)(2,1)} %param.7), channel_id=1, source_target_pairs={{0,14},{2,0},{4,2},{6,4},{8,6},{10,8},{12,10},{14,12},{1,15},{3,1}... | collective-permute-start | bytes 786440 | tf_op jit(solution)/shard_map/ppermute | solution.py:15
  36.3 18.1 %collective-permute-start.2 = (bf16[32,4096]{1,0:T(8,128)(2,1)S(1)}, bf16[32,4096]{1,0:T(8,128)(2,1)S(1)}, u32[]{:S(2)}, u32[]{:S(2)}) collective-permute-start(bf16[32,4096]{1,0:T(8,128)(2,1)S(1)} %collective-permute-done.1), channel_id=1, source_target_pairs={{0,2},{2,4},{4,6},{6,8},{8,10},{10,12},{12,14},{14,0},{1,3},{3,5},... | collective-permute-start | bytes 786440 | tf_op jit(solution)/shard_map/ppermute | solution.py:13
  41.6 17.6 %collective-permute-start.5 = (bf16[32,4096]{1,0:T(8,128)(2,1)S(1)}, bf16[32,4096]{1,0:T(8,128)(2,1)S(1)}, u32[]{:S(2)}, u32[]{:S(2)}) collective-permute-start(bf16[32,4096]{1,0:T(8,128)(2,1)S(1)} %collective-permute-done.4), channel_id=1, source_target_pairs={{0,14},{2,0},{4,2},{6,4},{8,6},{10,8},{12,10},{14,12},{1,15},{3,1}... | collective-permute-start | bytes 786440 | tf_op jit(solution)/shard_map/ppermute | solution.py:15
  54.4 14.6 %collective-permute-start.3 = (bf16[32,4096]{1,0:T(8,128)(2,1)S(1)}, bf16[32,4096]{1,0:T(8,128)(2,1)S(1)}, u32[]{:S(2)}, u32[]{:S(2)}) collective-permute-start(bf16[32,4096]{1,0:T(8,128)(2,1)S(1)} %collective-permute-done.2), channel_id=1, source_target_pairs={{0,2},{2,4},{4,6},{6,8},{8,10},{10,12},{12,14},{14,0},{1,3},{3,5},... | collective-permute-start | bytes 786440 | tf_op jit(solution)/shard_map/ppermute | solution.py:13
  59.2 15.9 %collective-permute-start.6 = (bf16[32,4096]{1,0:T(8,128)(2,1)S(1)}, bf16[32,4096]{1,0:T(8,128)(2,1)S(1)}, u32[]{:S(2)}, u32[]{:S(2)}) collective-permute-start(bf16[32,4096]{1,0:T(8,128)(2,1)S(1)} %collective-permute-done.5), channel_id=1, source_target_pairs={{0,14},{2,0},{4,2},{6,4},{8,6},{10,8},{12,10},{14,12},{1,15},{3,1}... | collective-permute-start | bytes 786440 | tf_op jit(solution)/shard_map/ppermute | solution.py:15
  81.7 79.3 %copy-start.7 = (bf16[192,128]{1,0:T(8,128)(2,1)S(1)}, bf16[192,128]{1,0:T(8,128)(2,1)}, u32[]{:S(2)}) copy-start(bf16[192,128]{1,0:T(8,128)(2,1)} %param.4) | copy-start | bytes 147460
  156.4 5.9 %copy-start.5 = (bf16[128,32768]{1,0:T(8,128)(2,1)S(1)}, bf16[128,32768]{1,0:T(8,128)(2,1)}, u32[]{:S(2)}) copy-start(bf16[128,32768]{1,0:T(8,128)(2,1)} %all-gather.2.cloned.1.call-done) | copy-start | bytes 25165828
  164.1 4.4 %copy-start = (bf16[192,8192]{1,0:T(8,128)(2,1)}, bf16[192,8192]{1,0:T(8,128)(2,1)S(1)}, u32[]{:S(2)}) copy-start(bf16[192,8192]{1,0:T(8,128)(2,1)S(1)} %fusion.18) | copy-start | bytes 9437188
  168.5 4.4 %copy-start.2 = (bf16[192,8192]{1,0:T(8,128)(2,1)}, bf16[192,8192]{1,0:T(8,128)(2,1)S(1)}, u32[]{:S(2)}) copy-start(bf16[192,8192]{1,0:T(8,128)(2,1)S(1)} %fusion.17) | copy-start | bytes 9437188
  172.9 4.4 %copy-start.4 = (bf16[192,8192]{1,0:T(8,128)(2,1)}, bf16[192,8192]{1,0:T(8,128)(2,1)S(1)}, u32[]{:S(2)}) copy-start(bf16[192,8192]{1,0:T(8,128)(2,1)S(1)} %fusion.19) | copy-start | bytes 9437188
  175.4 7.4 %copy-start.8 = (bf16[192,32]{0,1:T(8,128)(2,1)S(1)}, bf16[192,32]{0,1:T(8,128)(2,1)}, u32[]{:S(2)}) copy-start(bf16[192,32]{0,1:T(8,128)(2,1)} %param.5) | copy-start | bytes 36868
  182.9 2.8 %copy-start.1 = (bf16[192,8192]{1,0:T(8,128)(2,1)S(1)}, bf16[192,8192]{1,0:T(8,128)(2,1)}, u32[]{:S(2)}) copy-start(bf16[192,8192]{1,0:T(8,128)(2,1)} %copy-done) | copy-start | bytes 9437188
  182.9 3.8 %copy-start.3 = (bf16[192,8192]{1,0:T(8,128)(2,1)S(1)}, bf16[192,8192]{1,0:T(8,128)(2,1)}, u32[]{:S(2)}) copy-start(bf16[192,8192]{1,0:T(8,128)(2,1)} %copy-done.2) | copy-start | bytes 9437188
Sparse Core Ops, SparseCore 0:
  9.5 146.8 all-gather.1
  190.4 86.1 reduce-scatter.1
